TPU v7x, 32 devices: a whole 2x2x4 slice. The times are simulated.
32 devices in a mesh: row: 4 (over y, x), col: 8 (over z, core).
Axes of the slice: x: 2, y: 2, z: 4, core: 2. Of those that a mesh axis runs over, the one named last changes fastest.
Arguments:
- amplitudes: bfloat16 [4096, 4096], P('row', 'col'), may hold values from -6 to 6
- df_factors: bfloat16 [4096, 1024], P('col', 'row'), may hold values from -0.25 to 0.25
- ladder: bfloat16 [64, 64], P(('row', 'col')), may hold values from -0.75 to 0.75
- occ_energy: float32 [200], replicated, may hold values from -2.5 to -0.3
- occ_index: int32 [8], replicated, may hold values from 0 to 199
- vir_energy: float32 [512], replicated, may hold values from 0.3 to 3
- vir_map: int32 [512], replicated, may hold values from 0 to 511, each once
Outputs:
- residual_update: bfloat16 [4096, 4096], P('row', 'col')
All inputs are finite; a program needn't handle non-finite values.
Results may differ from a plain program's by a relative error of at most 0.0045.
The roundings to bfloat16 on the way count: a program that leaves them out, or rounds other values in their place, can miss the bound.
Values may be sent and summed in bfloat16 or wider, within the bound.
A program may use at most 64 MiB of HBM per device.

v0:
```python
import jax
import jax.numpy as jnp
from jax import lax
from jax.sharding import PartitionSpec as P

VIR = 512


def lookup(values, positions):
    table = jnp.arange(values.shape[0], dtype=jnp.int32)
    matches = positions[:, None] == table[None, :]
    return jnp.sum(jnp.where(matches, values[None, :], 0.0), axis=1)


def shards(amplitudes, df_factors, ladder, occ_energy, occ_index, vir_energy, vir_map):
    rows_tile, cols_tile = amplitudes.shape
    occ_row = rows_tile // VIR
    occ_col = cols_tile // VIR
    occ_all = occ_index.shape[0]
    vir_rows = VIR // lax.axis_size("row")
    vir_cols = VIR // lax.axis_size("col")
    blocks = amplitudes.reshape(occ_row, VIR, occ_col, VIR)
    mirror = jnp.transpose(blocks, (0, 3, 2, 1))
    combined = (2.0 * blocks.astype(jnp.float32) - mirror.astype(jnp.float32)).astype(jnp.bfloat16)
    combined = combined.reshape(rows_tile, cols_tile)
    factors = lax.all_gather(df_factors, "row", axis=1, tiled=True)
    partial_fit = jnp.dot(combined, factors, preferred_element_type=jnp.float32)
    contract = (((1,), (1,)), ((), ()))
    shared = lax.psum_scatter(partial_fit, "col", scatter_dimension=1, tiled=True).astype(
        jnp.bfloat16
    )
    fitted = lax.all_gather(shared, "col", axis=1, tiled=True)
    coulomb = lax.dot_general(fitted, factors, contract, preferred_element_type=jnp.float32)
    arranged = lax.all_to_all(
        lax.all_to_all(blocks, "row", split_axis=1, concat_axis=0, tiled=True),
        "col",
        split_axis=3,
        concat_axis=2,
        tiled=True,
    )
    pair_major = jnp.transpose(arranged, (0, 2, 1, 3)).reshape(
        occ_all * occ_all, vir_rows * vir_cols
    )
    hole_wide = jnp.dot(
        lax.all_gather(ladder, ("row", "col"), axis=0, tiled=True),
        pair_major,
        preferred_element_type=jnp.float32,
    )
    hole_term = hole_wide.astype(jnp.bfloat16)
    returned = jnp.transpose(hole_term.reshape(occ_all, occ_all, vir_rows, vir_cols), (0, 2, 1, 3))
    hole_tile = lax.all_to_all(
        lax.all_to_all(returned, "row", split_axis=0, concat_axis=1, tiled=True),
        "col",
        split_axis=2,
        concat_axis=3,
        tiled=True,
    )
    row_start = lax.axis_index("row") * occ_row
    col_start = lax.axis_index("col") * occ_col
    row_energy = lookup(occ_energy, lax.dynamic_slice_in_dim(occ_index, row_start, occ_row))
    col_energy = lookup(occ_energy, lax.dynamic_slice_in_dim(occ_index, col_start, occ_col))
    virtual = lookup(vir_energy, vir_map)
    denominator = (
        row_energy[:, None, None, None]
        + col_energy[None, None, :, None]
        - virtual[None, :, None, None]
        - virtual[None, None, None, :]
    )
    summed = coulomb.reshape(occ_row, VIR, occ_col, VIR) + hole_tile.astype(jnp.float32)
    return (summed / denominator).astype(jnp.bfloat16).reshape(rows_tile, cols_tile)


def solution(mesh):
    placed = (P("row", "col"), P("col", "row"), P(("row", "col"), None), P(), P(), P(), P())
    return jax.shard_map(
        shards, mesh=mesh, in_specs=placed, out_specs=P("row", "col"), check_vma=False
    )
```

profile of v0, /device:TPU:0, one launch (start us, length us, event | category | flops | bytes accessed | tf_op | source)
XLA Modules:
  0.0 222.1 jit_solution(15999204094148364111)
XLA Ops:
  7.3 1.5 copy.43
  8.8 1.3 fusion
  10.1 1.5 copy.44
  11.6 26.8 %all-gather.4.cloned.1.call-done = bf16[512,1024]{1,0:T(8,128)(2,1)} async-done(((bf16[512,256]{1,0:T(8,128)(2,1)}), bf16[512,1024]{1,0:T(8,128)(2,1)}) %all-gather.4.cloned.1.call-update) | async-done | bytes 1048592 | tf_op jit(solution)/shard_map/all_gather | solution.py:26
  38.4 4.5 %fusion.3 = f32[1024,1024]{1,0:T(8,128)} fusion(bf16[1024,512]{1,0:T(8,128)(2,1)S(1)} %bitcast.49, bf16[512,1024]{1,0:T(8,128)(2,1)} %all-gather.4.cloned.1.call-done), kind=kOutput, calls=%fused_computation.12 | convolution fusion | flops 1073741824 | bytes 6291456 | tf_op jit(solution)/shard_map/dot_general | solution.py:27
  42.9 1.1 copy.45
  44.0 16.8 %all_to_all.57 = bf16[2,512,1,512]{3,0,2,1:T(2,128)(2,1)S(1)} all-to-all(bf16[2,512,1,512]{3,0,2,1:T(2,128)(2,1)S(1)} %copy.45), channel_id=1, replica_groups=mesh['row'=4,'col'=8] {'row'}, dimensions={1} | all-to-all | bytes 2097152 | tf_op jit(solution)/shard_map/all_to_all | solution.py:35
  61.1 1.5 copy.48
  62.6 4.7 %all-to-all-start.1 = ((bf16[8,128,1,512]{1,0,2,3:T(8,128)(2,1)}), bf16[8,128,1,512]{1,0,2,3:T(8,128)(2,1)S(1)}, u32[]{:S(2)}, u32[]{:S(2)}) async-start(bf16[8,128,1,512]{1,0,2,3:T(8,128)(2,1)} %copy.48), calls=%async_computation.2 | async-start | bytes 2097152 | tf_op jit(solution)/shard_map/all_to_all | solution.py:34
  67.3 42.5 %reduce-scatter.2.cloned.1.call-done = f32[1024,128]{1,0:T(8,128)} async-done(((f32[1024,1024]{1,0:T(8,128)}), f32[1024,128]{1,0:T(8,128)}) %reduce-scatter.2.cloned.1.call-update) | async-done | bytes 524304 | tf_op jit(solution)/shard_map/reduce_scatter | solution.py:29
  109.8 1.8 convert_element_type.45
  111.6 40.3 %all-gather = bf16[32,2,64]{2,1,0:T(2,128)(2,1)S(1)} all-gather(bf16[1,2,64]{2,1,0:T(2,128)(2,1)S(1)} %bitcast.53), channel_id=1, replica_groups=mesh['row'=4,'col'=8] {'row','col'}, dimensions={0}, use_global_device_ids=true | all-gather | bytes 8448 | tf_op jit(solution)/shard_map/all_gather | solution.py:45
  151.9 1.2 copy.50
  153.1 1.7 reshape.103
  155.2 2.3 %reshape.104 = bf16[8,8,128,64]{3,2,1,0:T(8,128)(2,1)S(1)} reshape(bf16[64,8192]{1,0:T(8,128)(2,1)S(1)} %convolution_convert_fusion) | data formatting | bytes 2097152 | tf_op jit(solution)/shard_map/reshape | solution.py:50
  157.5 0.9 copy.51
  158.5 17.3 %all_to_all.58 = bf16[8,128,8,64]{1,3,2,0:T(8,128)(2,1)S(1)} all-to-all(bf16[8,128,8,64]{1,3,2,0:T(8,128)(2,1)S(1)} %copy.51), channel_id=1, replica_groups=mesh['row'=4,'col'=8] {'row'}, dimensions={0} | all-to-all | bytes 2097152 | tf_op jit(solution)/shard_map/all_to_all | solution.py:52
  175.8 0.8 copy.52
  176.6 1.2 all_to_all.51
  177.9 3.7 %all-to-all-start.3 = ((bf16[2,512,8,64]{1,0,3,2:T(2,128)(2,1)}), bf16[2,512,8,64]{1,0,3,2:T(2,128)(2,1)S(1)}, u32[]{:S(2)}, u32[]{:S(2)}) async-start(bf16[2,512,8,64]{1,0,3,2:T(2,128)(2,1)} %all_to_all.51), calls=%async_computation.4 | async-start | bytes 2097152 | tf_op jit(solution)/shard_map/all_to_all | solution.py:51
  182.3 1.1 fusion.2
  184.5 23.5 %all-to-all-done.3 = bf16[2,512,8,64]{1,0,3,2:T(2,128)(2,1)S(1)} async-done(((bf16[2,512,8,64]{1,0,3,2:T(2,128)(2,1)}), bf16[2,512,8,64]{1,0,3,2:T(2,128)(2,1)S(1)}, u32[]{:S(2)}, u32[]{:S(2)}) %all-to-all-start.3) | async-done | bytes 1048608 | tf_op jit(solution)/shard_map/all_to_all | solution.py:51
  209.2 1.9 copy.53
  211.0 4.5 %divide_convert_fusion = bf16[1024,512]{1,0:T(8,128)(2,1)} fusion(f32[1024,512]{1,0:T(8,128)} %copy.53, bf16[1024,1024]{1,0:T(8,128)(2,1)} %all-gather.6.cloned.1.call-done, bf16[512,1024]{1,0:T(8,128)(2,1)S(1)} %copy-done.5, f32[512]{0:T(512)S(1)} %select_reduce_fusion, f32[1024]{0:T(1024)S(1)} %sub.46), kind=kOutput, calls=%fused_computation.3 | convolution fusion | flops 1075838976 | bytes 6297600 | tf_op jit(solution)/shard_map/dot_general | solution.py:33
  (36 shorter events, 4.4 us)
Async XLA Ops:
  6.5 2.3 %copy-start = (bf16[1024,512]{1,0:T(8,128)(2,1)S(1)}, bf16[1024,512]{1,0:T(8,128)(2,1)}, u32[]{:S(2)}) copy-start(bf16[1024,512]{1,0:T(8,128)(2,1)} %param.7) | copy-start | bytes 3145732
  6.5 31.9 %all-gather.4.cloned.1.call-start = ((), (), s32[]{:S(2)}) async-start(), calls=%async_computation.5 | async-start | bytes 1310720 | tf_op jit(solution)/shard_map/all_gather | solution.py:26
  7.3 102.6 %reduce-scatter.2.cloned.1.call-start = ((), (), s32[]{:S(2)}) async-start(), calls=%async_computation.6 | async-start | bytes 4718592 | tf_op jit(solution)/shard_map/reduce_scatter | solution.py:29
  62.6 49.1 %copy-start.4 = (bf16[2,64]{1,0:T(2,128)(2,1)S(1)}, bf16[2,64]{1,0:T(2,128)(2,1)}, u32[]{:S(2)}) copy-start(bf16[2,64]{1,0:T(2,128)(2,1)} %param.9) | copy-start | bytes 772
  62.6 89.3 %all-to-all-start.1 = ((bf16[8,128,1,512]{1,0,2,3:T(8,128)(2,1)}), bf16[8,128,1,512]{1,0,2,3:T(8,128)(2,1)S(1)}, u32[]{:S(2)}, u32[]{:S(2)}) async-start(bf16[8,128,1,512]{1,0,2,3:T(8,128)(2,1)} %copy.48), calls=%async_computation.2 | async-start | bytes 2097152 | tf_op jit(solution)/shard_map/all_to_all | solution.py:34
  67.3 143.8 %all-gather.6.cloned.1.call-start = ((), (), s32[]{:S(2)}) async-start(), calls=%async_computation.7 | async-start | bytes 2359296 | tf_op jit(solution)/shard_map/all_gather | solution.py:32
  176.6 5.0 %copy-start.6 = (s32[8]{0:T(128)S(1)}, s32[8]{0:T(128)}, u32[]{:S(2)}) copy-start(s32[8]{0:T(128)} %param.11) | copy-start | bytes 100
  176.6 5.7 %copy-start.1 = (f32[200]{0:T(256)S(1)}, f32[200]{0:T(256)}, u32[]{:S(2)}) copy-start(f32[200]{0:T(256)} %param.10) | copy-start | bytes 2404
  176.6 7.6 %copy-start.2 = (f32[512]{0:T(512)S(1)}, f32[512]{0:T(512)}, u32[]{:S(2)}) copy-start(f32[512]{0:T(512)} %param.12) | copy-start | bytes 6148
  176.6 7.6 %copy-start.3 = (s32[512]{0:T(512)S(1)}, s32[512]{0:T(512)}, u32[]{:S(2)}) copy-start(s32[512]{0:T(512)} %param.13) | copy-start | bytes 6148
  177.9 30.1 %all-to-all-start.3 = ((bf16[2,512,8,64]{1,0,3,2:T(2,128)(2,1)}), bf16[2,512,8,64]{1,0,3,2:T(2,128)(2,1)S(1)}, u32[]{:S(2)}, u32[]{:S(2)}) async-start(bf16[2,512,8,64]{1,0,3,2:T(2,128)(2,1)} %all_to_all.51), calls=%async_computation.4 | async-start | bytes 2097152 | tf_op jit(solution)/shard_map/all_to_all | solution.py:51
  209.1 1.9 copy-start.5
Sparse Core Ops, SparseCore 0:
  9.2 29.1 all-gather.3
  43.0 66.7 reduce-scatter.1
  111.7 34.7 all-gather.5
where the time goes:
time: 223 us; the launch traced here: 222 us
  waiting for transfers between devices  93.5 us (42%)
  blocking collectives  74.4 us (33%)
  local copies, waits for them, and re-layouts  17 us (8%)
  between operations  13.3 us (6%)
  matrix products  9.38 us (4%)
  starting transfers between devices  8.55 us (4%)
  other arithmetic  5.93 us (3%)
    reduce_scatter x1, waiting for transfers between devices, shards(): lax.psum_scatter(partial_fit, 'col', scatter_dimension=1, tiled=True)  42.5 us
    all_gather x1, blocking collectives, shards(): lax.all_gather(ladder, ('row', 'col'), axis=0, tiled=True)  40.3 us
    all_gather x1, waiting for transfers between devices, shards(): factors = lax.all_gather(df_factors, 'row', axis=1, tiled=True)  26.8 us
    all_to_all x1, waiting for transfers between devices, shards(): lax.all_to_all(lax.all_to_all(returned, 'row', split_axis=0, concat_axis=...  23.5 us
    all_to_all x1, blocking collectives, shards(): lax.all_to_all(returned, 'row', split_axis=0, concat_axis=1, tiled=True)  17.3 us
    all_to_all x1, blocking collectives, shards(): lax.all_to_all(blocks, 'row', split_axis=1, concat_axis=0, tiled=True)  16.8 us
    all_to_all x1, starting transfers between devices, shards(): lax.all_to_all(lax.all_to_all(blocks, 'row', split_axis=1, concat_axis=0,...  4.74 us
    dot_general x1, matrix products, shards(): lax.dot_general(fitted, factors, contract, preferred_element_type=jnp.flo...  4.49 us
  transfers between devices with their start and end apart: 5, of which 3 were waited for; matrix products, arithmetic and copies ran while one was open for 10% of the time, Pallas kernels for 0%

commit v1 on v0

v1 whole, which is shorter than its diff:
```python
import functools

import jax
import jax.numpy as jnp
from jax import lax
from jax.experimental import pallas as pl
from jax.experimental.pallas import tpu as pltpu
from jax.sharding import PartitionSpec as P

VIR = 512
MESH = pl.DeviceIdType.MESH
F32 = jnp.float32
BF16 = jnp.bfloat16


def lookup(values, positions):
    table = jnp.arange(values.shape[0], dtype=jnp.int32)
    matches = positions[:, None] == table[None, :]
    return jnp.sum(jnp.where(matches, values[None, :], 0.0), axis=1)


def by_collectives(amplitudes, df_factors, ladder, occ_energy, occ_index, vir_energy, vir_map):
    rows_tile, cols_tile = amplitudes.shape
    occ_row = rows_tile // VIR
    occ_col = cols_tile // VIR
    occ_all = occ_index.shape[0]
    vir_rows = VIR // lax.axis_size("row")
    vir_cols = VIR // lax.axis_size("col")
    blocks = amplitudes.reshape(occ_row, VIR, occ_col, VIR)
    mirror = jnp.transpose(blocks, (0, 3, 2, 1))
    combined = (2.0 * blocks.astype(F32) - mirror.astype(F32)).astype(BF16)
    combined = combined.reshape(rows_tile, cols_tile)
    factors = lax.all_gather(df_factors, "row", axis=1, tiled=True)
    partial_fit = jnp.dot(combined, factors, preferred_element_type=F32)
    contract = (((1,), (1,)), ((), ()))
    shared = lax.psum_scatter(partial_fit, "col", scatter_dimension=1, tiled=True).astype(BF16)
    fitted = lax.all_gather(shared, "col", axis=1, tiled=True)
    coulomb = lax.dot_general(fitted, factors, contract, preferred_element_type=F32)
    arranged = lax.all_to_all(
        lax.all_to_all(blocks, "row", split_axis=1, concat_axis=0, tiled=True),
        "col",
        split_axis=3,
        concat_axis=2,
        tiled=True,
    )
    pair_major = jnp.transpose(arranged, (0, 2, 1, 3)).reshape(
        occ_all * occ_all, vir_rows * vir_cols
    )
    hole_wide = jnp.dot(
        lax.all_gather(ladder, ("row", "col"), axis=0, tiled=True),
        pair_major,
        preferred_element_type=F32,
    )
    hole_term = hole_wide.astype(BF16)
    returned = jnp.transpose(hole_term.reshape(occ_all, occ_all, vir_rows, vir_cols), (0, 2, 1, 3))
    hole_tile = lax.all_to_all(
        lax.all_to_all(returned, "row", split_axis=0, concat_axis=1, tiled=True),
        "col",
        split_axis=2,
        concat_axis=3,
        tiled=True,
    )
    row_start = lax.axis_index("row") * occ_row
    col_start = lax.axis_index("col") * occ_col
    row_energy = lookup(occ_energy, lax.dynamic_slice_in_dim(occ_index, row_start, occ_row))
    col_energy = lookup(occ_energy, lax.dynamic_slice_in_dim(occ_index, col_start, occ_col))
    virtual = lookup(vir_energy, vir_map)
    denominator = (
        row_energy[:, None, None, None]
        + col_energy[None, None, :, None]
        - virtual[None, :, None, None]
        - virtual[None, None, None, :]
    )
    summed = coulomb.reshape(occ_row, VIR, occ_col, VIR) + hole_tile.astype(F32)
    return (summed / denominator).astype(BF16).reshape(rows_tile, cols_tile)


def kernel(
    R, C, amp, fac, lad, occ_e, occ_i, vir_e, vir_m, out,
    comb, factors, part, twin, rs_out, rs_in, fit, pairs, hole, hole_in, kron, lad_own, lad_all,
    vcol,
    fac_s, fac_r, fwd_s, fwd_r, lad_s, lad_r, tw_s, tw_r, rs_s, rs_r, ag_s, ag_r, rl_s, rl_r,
    back_s, back_r,
):
    nd = R * C
    Z = C // 2
    occ_row, _, sub, _ = amp.shape
    rows = occ_row * VIR
    chunk = rows // C
    q_cols = fac.shape[1]
    per_pair = lad.shape[0]
    n_pairs = lad.shape[1]
    r = lax.axis_index("row")
    c = lax.axis_index("col")
    me = r * C + c
    core = lax.rem(c, 2)
    z = lax.div(c, 2)
    other = 1 - core

    def place(d):
        return (lax.div(d, C), lax.rem(d, C))

    def peer(o):
        return lax.rem(me + o, nd)

    def send(src, dst, s, d, target):
        return pltpu.make_async_remote_copy(
            src_ref=src, dst_ref=dst, send_sem=s, recv_sem=d, device_id=target, device_id_type=MESH
        )

    barrier = pltpu.get_barrier_semaphore()

    @pl.loop(1, nd)
    def _(o):
        pl.semaphore_signal(barrier, inc=1, device_id=place(peer(o)), device_id_type=MESH)

    pl.semaphore_wait(barrier, nd - 1)

    def fac_copy(o):
        return send(
            fac, factors.at[r], fac_s.at[o], fac_r.at[r], (lax.rem(r + o, R), c)
        )

    for o in range(1, R):
        fac_copy(o).start()

    lad_own[...] = jnp.zeros_like(lad_own)
    lad_own[0:per_pair, 0:n_pairs] = lad[...].astype(F32)

    def fwd_copy(o):
        d = peer(o)
        return send(amp.at[:, d], pairs.at[r, :, c], fwd_s.at[o], fwd_r.at[me], place(d))

    def lad_copy(o):
        return send(lad_own, lad_all.at[me], lad_s.at[o], lad_r.at[me], place(peer(o)))

    @pl.loop(1, nd)
    def _(o):
        fwd_copy(o).start()
        lad_copy(o).start()

    for k in range(occ_row):
        slab = amp[k].reshape(VIR, VIR).astype(F32)
        comb[k * VIR:(k + 1) * VIR, :] = (2.0 * slab - slab.T).astype(BF16)
    factors[r] = fac[...]
    pairs[r, :, c] = amp[:, me]
    lad_all[me] = lad_own[...]

    def tw_copy(q):
        return send(part.at[q, :, other], twin.at[q], tw_s.at[q], tw_r.at[q], (r, 2 * z + other))

    def rs_copy(o, q):
        to = lax.rem(z + o, Z)
        return send(
            rs_out.at[q, to], rs_in.at[q, z], rs_s.at[o, q], rs_r.at[q, z], (r, 2 * to + core)
        )

    for o in range(R):
        q = lax.rem(r + o, R)
        if o:
            send(fac, factors.at[q], fac_s.at[o], fac_r.at[q], (r, c)).wait_recv()
        got = jnp.dot(comb[...], factors[q], preferred_element_type=F32)
        part[q] = got.reshape(Z, 2, chunk, q_cols)
        tw_copy(q).start()

    for o in range(R):
        q = lax.rem(r + o, R)
        tw_copy(q).wait_recv()
        rs_out[q] = (part[q, :, core] + twin[q]).astype(BF16)
        for step in range(1, Z):
            rs_copy(step, q).start()

    ids_r = lax.broadcasted_iota(jnp.int32, (VIR, VIR), 0)
    ids_c = lax.broadcasted_iota(jnp.int32, (VIR, VIR), 1)
    e_col = jnp.sum(jnp.where(ids_r == ids_c, vir_e[...], 0.0), axis=1, keepdims=True)
    v_row = jnp.sum(jnp.where(ids_r == vir_m[...], e_col, 0.0), axis=0, keepdims=True)
    vcol[...] = jnp.sum(jnp.where(ids_r == ids_c, v_row, 0.0), axis=1, keepdims=True)

    @pl.loop(1, nd)
    def _(o):
        d = peer(o)
        send(lad_own, lad_all.at[d], lad_s.at[o], lad_r.at[d], place(d)).wait_recv()

    shift = sub.bit_length() - 1
    wide = n_pairs * sub
    lad_flat = lad_all[...].reshape(nd * lad_own.shape[0], lad_own.shape[1]).astype(BF16)
    spread = (
        lax.broadcasted_iota(jnp.int32, (lad_own.shape[1], wide), 0)
        == (lax.broadcasted_iota(jnp.int32, (lad_own.shape[1], wide), 1) >> shift)
    )
    lad_wide = jnp.dot(
        lad_flat, spread.astype(F32).astype(BF16), preferred_element_type=F32
    ).astype(BF16)
    step_rows = 128

    @pl.loop(0, wide // step_rows)
    def _(n):
        at = pl.multiple_of(n * step_rows, step_rows)
        pair = (lax.broadcasted_iota(jnp.int32, (step_rows, lad_flat.shape[0]), 0) + at) >> shift
        held = lax.broadcasted_iota(jnp.int32, (step_rows, lad_flat.shape[0]), 1)
        pick = held == (lax.div(pair, per_pair) * lad_own.shape[0] + lax.rem(pair, per_pair))
        block = jnp.dot(pick.astype(F32).astype(BF16), lad_wide, preferred_element_type=F32)
        same = (lax.broadcasted_iota(jnp.int32, (step_rows, wide), 0) & (sub - 1)) == (
            lax.broadcasted_iota(jnp.int32, (step_rows, wide), 1) & (sub - 1)
        )
        kron[pl.ds(at, step_rows), :] = jnp.where(same, block, 0.0).astype(BF16)

    @pl.loop(1, nd)
    def _(o):
        d = peer(o)
        dr, dc = place(d)
        send(amp.at[:, d], pairs.at[dr, :, dc], fwd_s.at[o], fwd_r.at[d], (dr, dc)).wait_recv()

    row_blocks = wide // R
    for n in range(R):
        term = jnp.dot(
            kron[n * row_blocks:(n + 1) * row_blocks, :],
            pairs[...].reshape(wide, VIR),
            preferred_element_type=F32,
        )
        hole[n] = term.astype(BF16).reshape(occ_row, C, sub, VIR)

    def back_copy(o):
        d = peer(o)
        dr, dc = place(d)
        return send(hole.at[dr, :, dc], hole_in.at[:, me], back_s.at[o], back_r.at[me], (dr, dc))

    @pl.loop(1, nd)
    def _(o):
        back_copy(o).start()

    hole_in[:, me] = hole[r, :, c]

    for o in range(R):
        q = lax.rem(r + o, R)
        total = part[q, z, core] + twin[q, z]
        for step in range(1, Z):
            src = lax.rem(z + step, Z)
            send(
                rs_out.at[q, src], rs_in.at[q, src], rs_s.at[step, q], rs_r.at[q, src], (r, c)
            ).wait_recv()
            total = total + rs_in[q, src].astype(F32)
        fit[z, core, q] = total.astype(BF16)

    def ag_copy(o):
        to = lax.rem(z + o, Z)
        return send(
            fit.at[z, core], fit.at[z, core], ag_s.at[o], ag_r.at[z], (r, 2 * to + core)
        )

    def relay(src):
        return send(
            fit.at[src, core], fit.at[src, core], rl_s.at[src], rl_r.at[src], (r, 2 * z + other)
        )

    for o in range(1, Z):
        ag_copy(o).start()
    relay(z).start()

    @pl.loop(1, nd)
    def _(o):
        d = peer(o)
        send(hole.at[r, :, c], hole_in.at[:, d], back_s.at[o], back_r.at[d], place(d)).wait_recv()

    per_occ = VIR // chunk
    groups = chunk // sub
    energy_j = occ_e[occ_i[c]]

    def finish(src, which):
        n = 2 * src + which
        k = lax.div(n, per_occ)
        m = lax.rem(n, per_occ)
        acc = None
        for q in range(R):
            term = lax.dot_general(
                fit[src, which, q], factors[q], (((1,), (1,)), ((), ())),
                preferred_element_type=F32,
            )
            acc = term if acc is None else acc + term
        held = hole_in[k, pl.ds(m * groups, groups)].reshape(chunk, VIR).astype(F32)
        energy = occ_e[occ_i[r * occ_row + k]] + energy_j
        rows_at = pl.multiple_of(m * chunk, chunk)
        denominator = (energy - vcol[pl.ds(rows_at, chunk), :]) - v_row
        at = pl.multiple_of(n * chunk, chunk)
        out[pl.ds(at, chunk), :] = ((acc + held) / denominator).astype(BF16)

    finish(z, core)
    for o in range(1, Z):
        src = lax.rem(z + o, Z)
        send(fit.at[src, core], fit.at[src, core], ag_s.at[o], ag_r.at[src], (r, c)).wait_recv()
        relay(src).start()
        finish(src, core)
    for o in range(Z):
        src = lax.rem(z + o, Z)
        send(
            fit.at[src, other], fit.at[src, other], rl_s.at[src], rl_r.at[src], (r, c)
        ).wait_recv()
        finish(src, other)

    @pl.loop(1, nd)
    def _(o):
        fwd_copy(o).wait_send()
        lad_copy(o).wait_send()
        back_copy(o).wait_send()

    for o in range(1, R):
        fac_copy(o).wait_send()
    for q in range(R):
        tw_copy(q).wait_send()
        for o in range(1, Z):
            rs_copy(o, q).wait_send()
    for o in range(1, Z):
        ag_copy(o).wait_send()
    for o in range(Z):
        relay(o).wait_send()


def fused(R, C, amplitudes, df_factors, ladder, occ_energy, occ_index, vir_energy, vir_map):
    nd = R * C
    Z = C // 2
    rows, _ = amplitudes.shape
    occ_row = rows // VIR
    sub = VIR // nd
    chunk = rows // C
    depth, q_cols = df_factors.shape
    n_pairs = ladder.shape[1]
    wide = n_pairs * sub
    lad_rows = -(-ladder.shape[0] // 8) * 8
    lad_cols = -(-n_pairs // 128) * 128
    vmem = pl.BlockSpec(memory_space=pltpu.VMEM)
    smem = pl.BlockSpec(memory_space=pltpu.SMEM)
    dma = pltpu.SemaphoreType.DMA
    return pl.pallas_call(
        functools.partial(kernel, R, C),
        out_shape=jax.ShapeDtypeStruct((rows, VIR), BF16),
        in_specs=[vmem, vmem, vmem, smem, smem, vmem, vmem],
        out_specs=vmem,
        scratch_shapes=[
            pltpu.VMEM((rows, VIR), BF16),
            pltpu.VMEM((R, depth, q_cols), BF16),
            pltpu.VMEM((R, Z, 2, chunk, q_cols), F32),
            pltpu.VMEM((R, Z, chunk, q_cols), F32),
            pltpu.VMEM((R, Z, chunk, q_cols), BF16),
            pltpu.VMEM((R, Z, chunk, q_cols), BF16),
            pltpu.VMEM((Z, 2, R, chunk, q_cols), BF16),
            pltpu.VMEM((R, occ_row, C, sub, VIR), BF16),
            pltpu.VMEM((R, occ_row, C, sub, VIR), BF16),
            pltpu.VMEM((occ_row, nd, sub, VIR), BF16),
            pltpu.VMEM((wide, wide), BF16),
            pltpu.VMEM((lad_rows, lad_cols), F32),
            pltpu.VMEM((nd, lad_rows, lad_cols), F32),
            pltpu.VMEM((VIR, 1), F32),
            dma((R,)), dma((R,)),
            dma((nd,)), dma((nd,)),
            dma((nd,)), dma((nd,)),
            dma((R,)), dma((R,)),
            dma((Z, R)), dma((R, Z)),
            dma((Z,)), dma((Z,)),
            dma((Z,)), dma((Z,)),
            dma((nd,)), dma((nd,)),
        ],
        compiler_params=pltpu.CompilerParams(
            collective_id=0, has_side_effects=True, vmem_limit_bytes=48 * 2**20
        ),
    )(
        amplitudes.reshape(occ_row, nd, sub, VIR), df_factors, ladder, occ_energy, occ_index,
        vir_energy.reshape(1, VIR), vir_map.reshape(1, VIR),
    )


def shards(amplitudes, df_factors, *rest):
    R, C = lax.axis_size("row"), lax.axis_size("col")
    rows, cols = amplitudes.shape
    fits = (
        VIR % (16 * R * C) == 0
        and cols == VIR
        and C % 2 == 0
        and rows % (16 * C) == 0
        and VIR % (rows // C) == 0
        and (rows // C) % (VIR // (R * C)) == 0
        and df_factors.shape[1] % 128 == 0
    )
    if fits:
        return fused(R, C, amplitudes, df_factors, *rest)
    return by_collectives(amplitudes, df_factors, *rest)


def solution(mesh):
    placed = (P("row", "col"), P("col", "row"), P(("row", "col"), None), P(), P(), P(), P())
    return jax.shard_map(
        shards, mesh=mesh, in_specs=placed, out_specs=P("row", "col"), check_vma=False
    )
```

time: 223 us -> 110 us (0.49)
  the two profiles are of different devices: /device:TPU:0 before, /device:TPU:9 now
where the time goes in v1:
time: 110 us
  Pallas kernels  106 us (96%)
  local copies, waits for them, and re-layouts  4.5 us (4%)
    pallas_call x1, Pallas kernels, fused(): pl.pallas_call(functools.partial(kernel, R, C), out_shape=jax.ShapeDtypeS...  106 us
    unnamed x15, local copies, waits for them, and re-layouts  4.5 us

profile of v1, /device:TPU:9, one launch (start us, length us, event | category | flops | bytes accessed | tf_op | source)
XLA Modules:
  0.0 110.2 jit_solution(15851251242877410022)
XLA Ops:
  0.0 0.0 copy-start.3
  0.0 0.0 copy-start.2
  0.0 0.0 copy-start.4
  0.0 0.0 copy-start.5
  0.0 0.7 copy-done.3
  0.7 0.0 copy-done.2
  0.7 0.0 copy-done.4
  0.7 0.0 copy-done.5
  0.7 0.0 copy-start
  0.7 1.2 %copy-done = bf16[1024,512]{1,0:T(8,128)(2,1)S(1)} copy-done((bf16[1024,512]{1,0:T(8,128)(2,1)S(1)}, bf16[1024,512]{1,0:T(8,128)(2,1)}, u32[]{:S(2)}) %copy-start) | copy-done | bytes 1048600
  1.9 0.0 copy-start.1
  1.9 0.9 copy-done.1
  2.9 0.0 copy-start.6
  2.9 0.7 copy-done.6
  3.5 105.7 %shard_map.73 = bf16[1024,512]{1,0:T(8,128)(2,1)S(1)} custom-call(bf16[2,32,16,512]{3,2,1,0:T(8,128)(2,1)S(1)} %bitcast.3, bf16[512,256]{1,0:T(8,128)(2,1)S(1)} %copy-done.1, bf16[2,64]{1,0:T(2,128)(2,1)S(1)} %copy-done.5, f32[200]{0:T(256)S(1)} %copy-done.4, s32[8]{0:T(128)S(1)} %copy-done.6, f32[1,512]{1,0:T(1,128)S(1)} %bitcast.4, s32[1,512]{1,0:T(1,128)S(1)} %bitcast.5), custom_call_target="tpu_custom_call" | custom-call | tf_op jit(solution)/shard_map/pallas_call | solution.py:333
  109.3 1.0 copy.9
Async XLA Ops:
  0.0 0.7 copy-start.3
  0.0 0.7 copy-start.2
  0.0 0.7 copy-start.4
  0.0 0.7 copy-start.5
  0.7 1.2 %copy-start = (bf16[1024,512]{1,0:T(8,128)(2,1)S(1)}, bf16[1024,512]{1,0:T(8,128)(2,1)}, u32[]{:S(2)}) copy-start(bf16[1024,512]{1,0:T(8,128)(2,1)} %param.7) | copy-start | bytes 3145732
  1.9 0.9 copy-start.1
  2.9 0.7 copy-start.6

commit v2 on v1

--- a/solution.py
+++ b/solution.py
@@ -77,10 +77,11 @@
 
 def kernel(
     R, C, amp, fac, lad, occ_e, occ_i, vir_e, vir_m, out,
-    comb, factors, part, twin, rs_out, rs_in, fit, pairs, hole, hole_in, kron, lad_own, lad_all,
-    vcol,
-    fac_s, fac_r, fwd_s, fwd_r, lad_s, lad_r, tw_s, tw_r, rs_s, rs_r, ag_s, ag_r, rl_s, rl_r,
-    back_s, back_r,
+    amp_v, lad_v, e_v, m_v, occ_ev, occ_iv, out_v,
+    comb, factors, part, twin, out1, in1, out2, in2, fit, pairs, hole, hole_in, kron, lad_own,
+    lad_all, vcol,
+    loc, put, fac_s, fac_r, fwd_s, fwd_r, lad_s, lad_r, tw_s, tw_r, s1_s, s1_r, s2_s, s2_r,
+    g1_s, g1_r, g2_s, g2_r, rl_s, rl_r, back_s, back_r,
 ):
     nd = R * C
     Z = C // 2
@@ -96,6 +97,9 @@
     core = lax.rem(c, 2)
     z = lax.div(c, 2)
     other = 1 - core
+    near = z + 1 - 2 * lax.rem(z, 2)
+    far = lax.rem(z + 2, Z)
+    far_near = lax.rem(near + 2, Z)
 
     def place(d):
         return (lax.div(d, C), lax.rem(d, C))
@@ -108,11 +112,26 @@
             src_ref=src, dst_ref=dst, send_sem=s, recv_sem=d, device_id=target, device_id_type=MESH
         )
 
+    own_copies = [
+        pltpu.make_async_copy(src, dst, loc.at[n])
+        for n, (src, dst) in enumerate((
+            (lad, lad_v), (amp, amp_v), (fac, factors.at[r]), (amp.at[:, me], pairs.at[r, :, c]),
+            (vir_e, e_v), (vir_m, m_v), (occ_e, occ_ev), (occ_i, occ_iv),
+        ))
+    ]
+    for copy in own_copies:
+        copy.start()
+
     barrier = pltpu.get_barrier_semaphore()
 
     @pl.loop(1, nd)
     def _(o):
         pl.semaphore_signal(barrier, inc=1, device_id=place(peer(o)), device_id_type=MESH)
+
+    lad_own[...] = jnp.zeros_like(lad_own)
+    own_copies[0].wait()
+    lad_own[0:per_pair, 0:n_pairs] = lad_v[...].astype(F32)
+    lad_all[me] = lad_own[...]
 
     pl.semaphore_wait(barrier, nd - 1)
 
@@ -124,9 +143,6 @@
     for o in range(1, R):
         fac_copy(o).start()
 
-    lad_own[...] = jnp.zeros_like(lad_own)
-    lad_own[0:per_pair, 0:n_pairs] = lad[...].astype(F32)
-
     def fwd_copy(o):
         d = peer(o)
         return send(amp.at[:, d], pairs.at[r, :, c], fwd_s.at[o], fwd_r.at[me], place(d))
@@ -139,41 +155,59 @@
         fwd_copy(o).start()
         lad_copy(o).start()
 
+    own_copies[1].wait()
     for k in range(occ_row):
-        slab = amp[k].reshape(VIR, VIR).astype(F32)
+        slab = amp_v[k].reshape(VIR, VIR).astype(F32)
         comb[k * VIR:(k + 1) * VIR, :] = (2.0 * slab - slab.T).astype(BF16)
-    factors[r] = fac[...]
-    pairs[r, :, c] = amp[:, me]
-    lad_all[me] = lad_own[...]
+    own_copies[2].wait()
 
     def tw_copy(q):
         return send(part.at[q, :, other], twin.at[q], tw_s.at[q], tw_r.at[q], (r, 2 * z + other))
 
-    def rs_copy(o, q):
-        to = lax.rem(z + o, Z)
+    def s1_copy(q):
+        return send(out1.at[q], in1.at[q], s1_s.at[q], s1_r.at[q], (r, 2 * near + core))
+
+    def s2_copy(q):
+        return send(out2.at[q], in2.at[q], s2_s.at[q], s2_r.at[q], (r, 2 * far + core))
+
+    def g1_copy(q):
         return send(
-            rs_out.at[q, to], rs_in.at[q, z], rs_s.at[o, q], rs_r.at[q, z], (r, 2 * to + core)
-        )
-
-    for o in range(R):
-        q = lax.rem(r + o, R)
+            fit.at[z, core, q], fit.at[z, core, q], g1_s.at[q], g1_r.at[q], (r, 2 * far + core)
+        )
+
+    def g2_copy(which, q):
+        src = far if which else z
+        return send(
+            fit.at[src, core, q], fit.at[src, core, q], g2_s.at[which, q], g2_r.at[which, q],
+            (r, 2 * near + core),
+        )
+
+    def relay(src):
+        return send(
+            fit.at[src, core], fit.at[src, core], rl_s.at[src], rl_r.at[src], (r, 2 * z + other)
+        )
+
+    order = [lax.rem(r + o, R) for o in range(R)]
+
+    for o, q in enumerate(order):
         if o:
             send(fac, factors.at[q], fac_s.at[o], fac_r.at[q], (r, c)).wait_recv()
         got = jnp.dot(comb[...], factors[q], preferred_element_type=F32)
         part[q] = got.reshape(Z, 2, chunk, q_cols)
         tw_copy(q).start()
 
-    for o in range(R):
-        q = lax.rem(r + o, R)
+    for q in order:
         tw_copy(q).wait_recv()
-        rs_out[q] = (part[q, :, core] + twin[q]).astype(BF16)
-        for step in range(1, Z):
-            rs_copy(step, q).start()
-
+        out1[q, 0] = (part[q, near, core] + twin[q, near]).astype(BF16)
+        out1[q, 1] = (part[q, far_near, core] + twin[q, far_near]).astype(BF16)
+        s1_copy(q).start()
+
+    for copy in own_copies[4:]:
+        copy.wait()
     ids_r = lax.broadcasted_iota(jnp.int32, (VIR, VIR), 0)
     ids_c = lax.broadcasted_iota(jnp.int32, (VIR, VIR), 1)
-    e_col = jnp.sum(jnp.where(ids_r == ids_c, vir_e[...], 0.0), axis=1, keepdims=True)
-    v_row = jnp.sum(jnp.where(ids_r == vir_m[...], e_col, 0.0), axis=0, keepdims=True)
+    e_col = jnp.sum(jnp.where(ids_r == ids_c, e_v[...], 0.0), axis=1, keepdims=True)
+    v_row = jnp.sum(jnp.where(ids_r == m_v[...], e_col, 0.0), axis=0, keepdims=True)
     vcol[...] = jnp.sum(jnp.where(ids_r == ids_c, v_row, 0.0), axis=1, keepdims=True)
 
     @pl.loop(1, nd)
@@ -205,6 +239,8 @@
         )
         kron[pl.ds(at, step_rows), :] = jnp.where(same, block, 0.0).astype(BF16)
 
+    own_copies[3].wait()
+
     @pl.loop(1, nd)
     def _(o):
         d = peer(o)
@@ -225,37 +261,45 @@
         dr, dc = place(d)
         return send(hole.at[dr, :, dc], hole_in.at[:, me], back_s.at[o], back_r.at[me], (dr, dc))
 
-    @pl.loop(1, nd)
+    @pl.loop(1, nd // 2)
     def _(o):
         back_copy(o).start()
 
+    for q in order:
+        s1_copy(q).wait_recv()
+        out2[q] = ((part[q, far, core] + twin[q, far]) + in1[q, 1].astype(F32)).astype(BF16)
+        s2_copy(q).start()
+
+    @pl.loop(nd // 2, nd)
+    def _(o):
+        back_copy(o).start()
+
     hole_in[:, me] = hole[r, :, c]
 
-    for o in range(R):
-        q = lax.rem(r + o, R)
-        total = part[q, z, core] + twin[q, z]
-        for step in range(1, Z):
-            src = lax.rem(z + step, Z)
-            send(
-                rs_out.at[q, src], rs_in.at[q, src], rs_s.at[step, q], rs_r.at[q, src], (r, c)
-            ).wait_recv()
-            total = total + rs_in[q, src].astype(F32)
-        fit[z, core, q] = total.astype(BF16)
-
-    def ag_copy(o):
-        to = lax.rem(z + o, Z)
-        return send(
-            fit.at[z, core], fit.at[z, core], ag_s.at[o], ag_r.at[z], (r, 2 * to + core)
-        )
-
-    def relay(src):
-        return send(
-            fit.at[src, core], fit.at[src, core], rl_s.at[src], rl_r.at[src], (r, 2 * z + other)
-        )
-
-    for o in range(1, Z):
-        ag_copy(o).start()
+    for q in order:
+        s2_copy(q).wait_recv()
+        total = (part[q, z, core] + twin[q, z]) + in1[q, 0].astype(F32)
+        fit[z, core, q] = (total + in2[q].astype(F32)).astype(BF16)
+        g1_copy(q).start()
+        g2_copy(0, q).start()
     relay(z).start()
+
+    def g1_wait(q):
+        send(
+            fit.at[far, core, q], fit.at[far, core, q], g1_s.at[q], g1_r.at[q], (r, c)
+        ).wait_recv()
+
+    def g2_wait(which, q):
+        src = far_near if which else near
+        send(
+            fit.at[src, core, q], fit.at[src, core, q], g2_s.at[which, q], g2_r.at[which, q],
+            (r, c),
+        ).wait_recv()
+
+    for q in order:
+        g1_wait(q)
+        g2_copy(1, q).start()
+    relay(far).start()
 
     @pl.loop(1, nd)
     def _(o):
@@ -264,7 +308,11 @@
 
     per_occ = VIR // chunk
     groups = chunk // sub
-    energy_j = occ_e[occ_i[c]]
+    energy_j = occ_ev[occ_iv[c]]
+
+    def out_copy(n):
+        at = pl.ds(pl.multiple_of(n * chunk, chunk), chunk)
+        return pltpu.make_async_copy(out_v.at[at, :], out.at[at, :], put.at[n])
 
     def finish(src, which):
         n = 2 * src + which
@@ -278,23 +326,32 @@
             )
             acc = term if acc is None else acc + term
         held = hole_in[k, pl.ds(m * groups, groups)].reshape(chunk, VIR).astype(F32)
-        energy = occ_e[occ_i[r * occ_row + k]] + energy_j
+        energy = occ_ev[occ_iv[r * occ_row + k]] + energy_j
         rows_at = pl.multiple_of(m * chunk, chunk)
         denominator = (energy - vcol[pl.ds(rows_at, chunk), :]) - v_row
         at = pl.multiple_of(n * chunk, chunk)
-        out[pl.ds(at, chunk), :] = ((acc + held) / denominator).astype(BF16)
-
-    finish(z, core)
-    for o in range(1, Z):
-        src = lax.rem(z + o, Z)
-        send(fit.at[src, core], fit.at[src, core], ag_s.at[o], ag_r.at[src], (r, c)).wait_recv()
-        relay(src).start()
-        finish(src, core)
-    for o in range(Z):
-        src = lax.rem(z + o, Z)
+        out_v[pl.ds(at, chunk), :] = ((acc + held) / denominator).astype(BF16)
+        out_copy(n).start()
+
+    def relay_wait(src):
         send(
             fit.at[src, other], fit.at[src, other], rl_s.at[src], rl_r.at[src], (r, c)
         ).wait_recv()
+
+    finish(z, core)
+    finish(far, core)
+    relay_wait(z)
+    finish(z, other)
+    for which, src in ((0, near), (1, far_near)):
+        for q in order:
+            g2_wait(which, q)
+        relay(src).start()
+        finish(src, core)
+        if which == 0:
+            relay_wait(far)
+            finish(far, other)
+    for src in (near, far_near):
+        relay_wait(src)
         finish(src, other)
 
     @pl.loop(1, nd)
@@ -307,12 +364,15 @@
         fac_copy(o).wait_send()
     for q in range(R):
         tw_copy(q).wait_send()
-        for o in range(1, Z):
-            rs_copy(o, q).wait_send()
-    for o in range(1, Z):
-        ag_copy(o).wait_send()
+        s1_copy(q).wait_send()
+        s2_copy(q).wait_send()
+        g1_copy(q).wait_send()
+        g2_copy(0, q).wait_send()
+        g2_copy(1, q).wait_send()
     for o in range(Z):
         relay(o).wait_send()
+    for n in range(C):
+        out_copy(n).wait()
 
 
 def fused(R, C, amplitudes, df_factors, ladder, occ_energy, occ_index, vir_energy, vir_map):
@@ -327,21 +387,29 @@
     wide = n_pairs * sub
     lad_rows = -(-ladder.shape[0] // 8) * 8
     lad_cols = -(-n_pairs // 128) * 128
-    vmem = pl.BlockSpec(memory_space=pltpu.VMEM)
-    smem = pl.BlockSpec(memory_space=pltpu.SMEM)
+    hbm = pl.BlockSpec(memory_space=pl.ANY)
     dma = pltpu.SemaphoreType.DMA
     return pl.pallas_call(
         functools.partial(kernel, R, C),
         out_shape=jax.ShapeDtypeStruct((rows, VIR), BF16),
-        in_specs=[vmem, vmem, vmem, smem, smem, vmem, vmem],
-        out_specs=vmem,
+        in_specs=[hbm] * 7,
+        out_specs=hbm,
         scratch_shapes=[
+            pltpu.VMEM((occ_row, nd, sub, VIR), BF16),
+            pltpu.VMEM(ladder.shape, BF16),
+            pltpu.VMEM((1, VIR), F32),
+            pltpu.VMEM((1, VIR), jnp.int32),
+            pltpu.SMEM(occ_energy.shape, F32),
+            pltpu.SMEM(occ_index.shape, jnp.int32),
+            pltpu.VMEM((rows, VIR), BF16),
             pltpu.VMEM((rows, VIR), BF16),
             pltpu.VMEM((R, depth, q_cols), BF16),
             pltpu.VMEM((R, Z, 2, chunk, q_cols), F32),
             pltpu.VMEM((R, Z, chunk, q_cols), F32),
-            pltpu.VMEM((R, Z, chunk, q_cols), BF16),
-            pltpu.VMEM((R, Z, chunk, q_cols), BF16),
+            pltpu.VMEM((R, 2, chunk, q_cols), BF16),
+            pltpu.VMEM((R, 2, chunk, q_cols), BF16),
+            pltpu.VMEM((R, chunk, q_cols), BF16),
+            pltpu.VMEM((R, chunk, q_cols), BF16),
             pltpu.VMEM((Z, 2, R, chunk, q_cols), BF16),
             pltpu.VMEM((R, occ_row, C, sub, VIR), BF16),
             pltpu.VMEM((R, occ_row, C, sub, VIR), BF16),
@@ -350,17 +418,20 @@
             pltpu.VMEM((lad_rows, lad_cols), F32),
             pltpu.VMEM((nd, lad_rows, lad_cols), F32),
             pltpu.VMEM((VIR, 1), F32),
+            dma((8,)), dma((C,)),
             dma((R,)), dma((R,)),
             dma((nd,)), dma((nd,)),
             dma((nd,)), dma((nd,)),
             dma((R,)), dma((R,)),
-            dma((Z, R)), dma((R, Z)),
-            dma((Z,)), dma((Z,)),
+            dma((R,)), dma((R,)),
+            dma((R,)), dma((R,)),
+            dma((R,)), dma((R,)),
+            dma((2, R)), dma((2, R)),
             dma((Z,)), dma((Z,)),
             dma((nd,)), dma((nd,)),
         ],
         compiler_params=pltpu.CompilerParams(
-            collective_id=0, has_side_effects=True, vmem_limit_bytes=48 * 2**20
+            collective_id=0, has_side_effects=True, vmem_limit_bytes=56 * 2**20
         ),
     )(
         amplitudes.reshape(occ_row, nd, sub, VIR), df_factors, ladder, occ_energy, occ_index,
@@ -374,7 +445,7 @@
     fits = (
         VIR % (16 * R * C) == 0
         and cols == VIR
-        and C % 2 == 0
+        and C == 8
         and rows % (16 * C) == 0
         and VIR % (rows // C) == 0
         and (rows // C) % (VIR // (R * C)) == 0

time: 110 us -> 95.9 us (0.87)
  the two profiles are of different devices: /device:TPU:9 before, /device:TPU:0 now
where the time goes in v2:
time: 95.9 us; the launch traced here: 94.2 us
  Pallas kernels  91.9 us (96%)
  local copies, waits for them, and re-layouts  2.26 us (2%)
    pallas_call x1, Pallas kernels, fused(): pl.pallas_call(functools.partial(kernel, R, C), out_shape=jax.ShapeDtypeS...  91.9 us
    unnamed x1, local copies, waits for them, and re-layouts  2.26 us

profile of v2, /device:TPU:0, one launch (start us, length us, event | category | flops | bytes accessed | tf_op | source)
XLA Modules:
  0.0 94.2 jit_solution(9767976728017533135)
XLA Ops:
  0.0 91.9 %shard_map.73 = bf16[1024,512]{1,0:T(8,128)(2,1)} custom-call(bf16[2,32,16,512]{3,2,1,0:T(8,128)(2,1)} %bitcast.3, bf16[512,256]{1,0:T(8,128)(2,1)} %fac.1, bf16[2,64]{1,0:T(2,128)(2,1)} %lad.1, f32[200]{0:T(256)} %occ_e.1, s32[8]{0:T(128)} %occ_i.1, f32[1,512]{1,0:T(1,128)} %bitcast.4, s32[1,512]{1,0:T(1,128)} %bitcast.5), custom_call_target="tpu_custom_call" | custom-call | tf_op jit(solution)/shard_map/pallas_call | solution.py:392
  91.9 2.3 %copy.9 = bf16[1024,512]{1,0:T(8,128)(2,1)} copy(bf16[1024,512]{1,0:T(8,128)(2,1)} %shard_map.73) | data formatting | bytes 2097152

commit v3 on v2

--- a/solution.py
+++ b/solution.py
@@ -77,10 +77,10 @@
 
 def kernel(
     R, C, amp, fac, lad, occ_e, occ_i, vir_e, vir_m, out,
-    amp_v, lad_v, e_v, m_v, occ_ev, occ_iv, out_v,
+    amp_v, lad_v, e_v, m_v, occ_ev, occ_iv,
     comb, factors, part, twin, out1, in1, out2, in2, fit, pairs, hole, hole_in, kron, lad_own,
-    lad_all, vcol,
-    loc, put, fac_s, fac_r, fwd_s, fwd_r, lad_s, lad_r, tw_s, tw_r, s1_s, s1_r, s2_s, s2_r,
+    lad_all, inverse, coul,
+    loc, fac_s, fac_r, fwd_s, fwd_r, lad_s, lad_r, tw_s, tw_r, s1_s, s1_r, s2_s, s2_r,
     g1_s, g1_r, g2_s, g2_r, rl_s, rl_r, back_s, back_r,
 ):
     nd = R * C
@@ -150,10 +150,19 @@
     def lad_copy(o):
         return send(lad_own, lad_all.at[me], lad_s.at[o], lad_r.at[me], place(peer(o)))
 
-    @pl.loop(1, nd)
-    def _(o):
-        fwd_copy(o).start()
+    def fwd_start(lo, hi):
+        @pl.loop(lo, hi)
+        def _(o):
+            fwd_copy(o).start()
+
+    first = nd // 2
+    batch = -(-(nd - first) // R)
+
+    @pl.loop(1, nd)
+    def _(o):
         lad_copy(o).start()
+
+    fwd_start(1, first)
 
     own_copies[1].wait()
     for k in range(occ_row):
@@ -196,11 +205,12 @@
         part[q] = got.reshape(Z, 2, chunk, q_cols)
         tw_copy(q).start()
 
-    for q in order:
+    for o, q in enumerate(order):
         tw_copy(q).wait_recv()
         out1[q, 0] = (part[q, near, core] + twin[q, near]).astype(BF16)
         out1[q, 1] = (part[q, far_near, core] + twin[q, far_near]).astype(BF16)
         s1_copy(q).start()
+        fwd_start(first + o * batch, min(first + (o + 1) * batch, nd))
 
     for copy in own_copies[4:]:
         copy.wait()
@@ -208,7 +218,11 @@
     ids_c = lax.broadcasted_iota(jnp.int32, (VIR, VIR), 1)
     e_col = jnp.sum(jnp.where(ids_r == ids_c, e_v[...], 0.0), axis=1, keepdims=True)
     v_row = jnp.sum(jnp.where(ids_r == m_v[...], e_col, 0.0), axis=0, keepdims=True)
-    vcol[...] = jnp.sum(jnp.where(ids_r == ids_c, v_row, 0.0), axis=1, keepdims=True)
+    v_col = jnp.sum(jnp.where(ids_r == ids_c, v_row, 0.0), axis=1, keepdims=True)
+    energy_j = occ_ev[occ_iv[c]]
+    for k in range(occ_row):
+        energy = occ_ev[occ_iv[r * occ_row + k]] + energy_j
+        inverse[k * VIR:(k + 1) * VIR, :] = 1.0 / ((energy - v_col) - v_row)
 
     @pl.loop(1, nd)
     def _(o):
@@ -261,27 +275,34 @@
         dr, dc = place(d)
         return send(hole.at[dr, :, dc], hole_in.at[:, me], back_s.at[o], back_r.at[me], (dr, dc))
 
-    @pl.loop(1, nd // 2)
-    def _(o):
-        back_copy(o).start()
-
-    for q in order:
+    def back_start(lo, hi):
+        @pl.loop(lo, hi)
+        def _(o):
+            back_copy(o).start()
+
+    first = nd // 4
+    batch = -(-(nd - first) // (2 * R))
+
+    def back_batch(n):
+        back_start(first + n * batch, min(first + (n + 1) * batch, nd))
+
+    back_start(1, first)
+
+    for o, q in enumerate(order):
         s1_copy(q).wait_recv()
         out2[q] = ((part[q, far, core] + twin[q, far]) + in1[q, 1].astype(F32)).astype(BF16)
         s2_copy(q).start()
-
-    @pl.loop(nd // 2, nd)
-    def _(o):
-        back_copy(o).start()
+        back_batch(o)
 
     hole_in[:, me] = hole[r, :, c]
 
-    for q in order:
+    for o, q in enumerate(order):
         s2_copy(q).wait_recv()
         total = (part[q, z, core] + twin[q, z]) + in1[q, 0].astype(F32)
         fit[z, core, q] = (total + in2[q].astype(F32)).astype(BF16)
         g1_copy(q).start()
         g2_copy(0, q).start()
+        back_batch(R + o)
     relay(z).start()
 
     def g1_wait(q):
@@ -296,28 +317,13 @@
             (r, c),
         ).wait_recv()
 
-    for q in order:
-        g1_wait(q)
-        g2_copy(1, q).start()
-    relay(far).start()
-
-    @pl.loop(1, nd)
-    def _(o):
-        d = peer(o)
-        send(hole.at[r, :, c], hole_in.at[:, d], back_s.at[o], back_r.at[d], place(d)).wait_recv()
-
     per_occ = VIR // chunk
     groups = chunk // sub
-    energy_j = occ_ev[occ_iv[c]]
-
-    def out_copy(n):
-        at = pl.ds(pl.multiple_of(n * chunk, chunk), chunk)
-        return pltpu.make_async_copy(out_v.at[at, :], out.at[at, :], put.at[n])
-
-    def finish(src, which):
-        n = 2 * src + which
-        k = lax.div(n, per_occ)
-        m = lax.rem(n, per_occ)
+
+    def rows_of(n):
+        return pl.ds(pl.multiple_of(n * chunk, chunk), chunk)
+
+    def fitted_dot(src, which):
         acc = None
         for q in range(R):
             term = lax.dot_general(
@@ -325,34 +331,48 @@
                 preferred_element_type=F32,
             )
             acc = term if acc is None else acc + term
+        return acc
+
+    def finish(src, which, acc):
+        n = 2 * src + which
+        k = lax.div(n, per_occ)
+        m = lax.rem(n, per_occ)
         held = hole_in[k, pl.ds(m * groups, groups)].reshape(chunk, VIR).astype(F32)
-        energy = occ_ev[occ_iv[r * occ_row + k]] + energy_j
-        rows_at = pl.multiple_of(m * chunk, chunk)
-        denominator = (energy - vcol[pl.ds(rows_at, chunk), :]) - v_row
-        at = pl.multiple_of(n * chunk, chunk)
-        out_v[pl.ds(at, chunk), :] = ((acc + held) / denominator).astype(BF16)
-        out_copy(n).start()
+        out[rows_of(n), :] = ((acc + held) * inverse[rows_of(n), :]).astype(BF16)
 
     def relay_wait(src):
         send(
             fit.at[src, other], fit.at[src, other], rl_s.at[src], rl_r.at[src], (r, c)
         ).wait_recv()
 
-    finish(z, core)
-    finish(far, core)
+    coul[0] = fitted_dot(z, core)
+    for q in order:
+        g1_wait(q)
+        g2_copy(1, q).start()
+    relay(far).start()
+    coul[1] = fitted_dot(far, core)
     relay_wait(z)
-    finish(z, other)
+    coul[2] = fitted_dot(z, other)
+    relay_wait(far)
+    coul[3] = fitted_dot(far, other)
+
+    @pl.loop(1, nd)
+    def _(o):
+        d = peer(o)
+        send(hole.at[r, :, c], hole_in.at[:, d], back_s.at[o], back_r.at[d], place(d)).wait_recv()
+
+    finish(z, core, coul[0])
+    finish(far, core, coul[1])
+    finish(z, other, coul[2])
+    finish(far, other, coul[3])
     for which, src in ((0, near), (1, far_near)):
         for q in order:
             g2_wait(which, q)
         relay(src).start()
-        finish(src, core)
-        if which == 0:
-            relay_wait(far)
-            finish(far, other)
+        finish(src, core, fitted_dot(src, core))
     for src in (near, far_near):
         relay_wait(src)
-        finish(src, other)
+        finish(src, other, fitted_dot(src, other))
 
     @pl.loop(1, nd)
     def _(o):
@@ -371,8 +391,6 @@
         g2_copy(1, q).wait_send()
     for o in range(Z):
         relay(o).wait_send()
-    for n in range(C):
-        out_copy(n).wait()
 
 
 def fused(R, C, amplitudes, df_factors, ladder, occ_energy, occ_index, vir_energy, vir_map):
@@ -393,7 +411,7 @@
         functools.partial(kernel, R, C),
         out_shape=jax.ShapeDtypeStruct((rows, VIR), BF16),
         in_specs=[hbm] * 7,
-        out_specs=hbm,
+        out_specs=pl.BlockSpec(memory_space=pltpu.VMEM),
         scratch_shapes=[
             pltpu.VMEM((occ_row, nd, sub, VIR), BF16),
             pltpu.VMEM(ladder.shape, BF16),
@@ -401,7 +419,6 @@
             pltpu.VMEM((1, VIR), jnp.int32),
             pltpu.SMEM(occ_energy.shape, F32),
             pltpu.SMEM(occ_index.shape, jnp.int32),
-            pltpu.VMEM((rows, VIR), BF16),
             pltpu.VMEM((rows, VIR), BF16),
             pltpu.VMEM((R, depth, q_cols), BF16),
             pltpu.VMEM((R, Z, 2, chunk, q_cols), F32),
@@ -417,8 +434,9 @@
             pltpu.VMEM((wide, wide), BF16),
             pltpu.VMEM((lad_rows, lad_cols), F32),
             pltpu.VMEM((nd, lad_rows, lad_cols), F32),
-            pltpu.VMEM((VIR, 1), F32),
-            dma((8,)), dma((C,)),
+            pltpu.VMEM((rows, VIR), F32),
+            pltpu.VMEM((4, chunk, VIR), F32),
+            dma((8,)),
             dma((R,)), dma((R,)),
             dma((nd,)), dma((nd,)),
             dma((nd,)), dma((nd,)),

time: 95.9 us -> 110 us (1.15)
  Pallas kernels: 91.9 us -> 106 us
    pallas_call x1, Pallas kernels: 91.9 us -> 106 us  [fused(): pl.pallas_call(functools.partial(kernel, R, C), out_shape=jax.ShapeDtypeS...]
where the time goes in v3:
time: 110 us; the launch traced here: 108 us
  Pallas kernels  106 us (96%)
  local copies, waits for them, and re-layouts  2.26 us (2%)
    pallas_call x1, Pallas kernels, fused(): pl.pallas_call(functools.partial(kernel, R, C), out_shape=jax.ShapeDtypeS...  106 us
    unnamed x1, local copies, waits for them, and re-layouts  2.26 us

profile of v3, /device:TPU:0, one launch (start us, length us, event | category | flops | bytes accessed | tf_op | source)
XLA Modules:
  0.0 107.9 jit_solution(6327151982070813710)
XLA Ops:
  0.0 105.6 %shard_map.73 = bf16[1024,512]{1,0:T(8,128)(2,1)} custom-call(bf16[2,32,16,512]{3,2,1,0:T(8,128)(2,1)} %bitcast.3, bf16[512,256]{1,0:T(8,128)(2,1)} %fac.1, bf16[2,64]{1,0:T(2,128)(2,1)} %lad.1, f32[200]{0:T(256)} %occ_e.1, s32[8]{0:T(128)} %occ_i.1, f32[1,512]{1,0:T(1,128)} %bitcast.4, s32[1,512]{1,0:T(1,128)} %bitcast.5), custom_call_target="tpu_custom_call" | custom-call | tf_op jit(solution)/shard_map/pallas_call | solution.py:410
  105.6 2.3 %copy.9 = bf16[1024,512]{1,0:T(8,128)(2,1)} copy(bf16[1024,512]{1,0:T(8,128)(2,1)} %shard_map.73) | data formatting | bytes 2097152

commit v4 on v3

--- a/solution.py
+++ b/solution.py
@@ -105,7 +105,7 @@
         return (lax.div(d, C), lax.rem(d, C))
 
     def peer(o):
-        return lax.rem(me + o, nd)
+        return lax.rem(r + lax.div(o, C), R) * C + lax.rem(c + lax.rem(o, C), C)
 
     def send(src, dst, s, d, target):
         return pltpu.make_async_remote_copy(
@@ -155,14 +155,7 @@
         def _(o):
             fwd_copy(o).start()
 
-    first = nd // 2
-    batch = -(-(nd - first) // R)
-
-    @pl.loop(1, nd)
-    def _(o):
-        lad_copy(o).start()
-
-    fwd_start(1, first)
+    fwd_start(1, C)
 
     own_copies[1].wait()
     for k in range(occ_row):
@@ -204,13 +197,18 @@
         got = jnp.dot(comb[...], factors[q], preferred_element_type=F32)
         part[q] = got.reshape(Z, 2, chunk, q_cols)
         tw_copy(q).start()
-
-    for o, q in enumerate(order):
+        if o == 0:
+            fwd_start(C, nd)
+
+            @pl.loop(1, nd)
+            def _(n):
+                lad_copy(n).start()
+
+    for q in order:
         tw_copy(q).wait_recv()
         out1[q, 0] = (part[q, near, core] + twin[q, near]).astype(BF16)
         out1[q, 1] = (part[q, far_near, core] + twin[q, far_near]).astype(BF16)
         s1_copy(q).start()
-        fwd_start(first + o * batch, min(first + (o + 1) * batch, nd))
 
     for copy in own_copies[4:]:
         copy.wait()
@@ -275,34 +273,23 @@
         dr, dc = place(d)
         return send(hole.at[dr, :, dc], hole_in.at[:, me], back_s.at[o], back_r.at[me], (dr, dc))
 
-    def back_start(lo, hi):
-        @pl.loop(lo, hi)
-        def _(o):
-            back_copy(o).start()
-
-    first = nd // 4
-    batch = -(-(nd - first) // (2 * R))
-
-    def back_batch(n):
-        back_start(first + n * batch, min(first + (n + 1) * batch, nd))
-
-    back_start(1, first)
-
-    for o, q in enumerate(order):
+    @pl.loop(1, nd)
+    def _(o):
+        back_copy(o).start()
+
+    for q in order:
         s1_copy(q).wait_recv()
         out2[q] = ((part[q, far, core] + twin[q, far]) + in1[q, 1].astype(F32)).astype(BF16)
         s2_copy(q).start()
-        back_batch(o)
 
     hole_in[:, me] = hole[r, :, c]
 
-    for o, q in enumerate(order):
+    for q in order:
         s2_copy(q).wait_recv()
         total = (part[q, z, core] + twin[q, z]) + in1[q, 0].astype(F32)
         fit[z, core, q] = (total + in2[q].astype(F32)).astype(BF16)
         g1_copy(q).start()
         g2_copy(0, q).start()
-        back_batch(R + o)
     relay(z).start()
 
     def g1_wait(q):
@@ -449,7 +436,7 @@
             dma((nd,)), dma((nd,)),
         ],
         compiler_params=pltpu.CompilerParams(
-            collective_id=0, has_side_effects=True, vmem_limit_bytes=56 * 2**20
+            collective_id=0, has_side_effects=True, vmem_limit_bytes=40 * 2**20
         ),
     )(
         amplitudes.reshape(occ_row, nd, sub, VIR), df_factors, ladder, occ_energy, occ_index,

time: 110 us -> 98.8 us (0.90); the launches traced: 108 us -> 98.6 us
  Pallas kernels: 106 us -> 94 us
  local copies, waits for them, and re-layouts: 2.26 us -> 4.51 us
    pallas_call x1, Pallas kernels: 106 us -> 94 us  [fused(): pl.pallas_call(functools.partial(kernel, R, C), out_shape=jax.ShapeDtypeS...]
    unnamed x1 -> x15, local copies, waits for them, and re-layouts: 2.26 us -> 4.51 us
where the time goes in v4:
time: 98.8 us; the launch traced here: 98.6 us
  Pallas kernels  94 us (95%)
  local copies, waits for them, and re-layouts  4.51 us (5%)
    pallas_call x1, Pallas kernels, fused(): pl.pallas_call(functools.partial(kernel, R, C), out_shape=jax.ShapeDtypeS...  94 us
    unnamed x15, local copies, waits for them, and re-layouts  4.51 us

profile of v4, /device:TPU:0, one launch (start us, length us, event | category | flops | bytes accessed | tf_op | source)
XLA Modules:
  0.0 98.6 jit_solution(9640452942279217676)
XLA Ops:
  0.0 0.0 copy-start.3
  0.0 0.0 copy-start.2
  0.0 0.0 copy-start.4
  0.0 0.0 copy-start.5
  0.0 0.7 copy-done.3
  0.7 0.0 copy-done.2
  0.7 0.0 copy-done.4
  0.7 0.0 copy-done.5
  0.7 0.0 copy-start
  0.7 1.2 %copy-done = bf16[1024,512]{1,0:T(8,128)(2,1)S(1)} copy-done((bf16[1024,512]{1,0:T(8,128)(2,1)S(1)}, bf16[1024,512]{1,0:T(8,128)(2,1)}, u32[]{:S(2)}) %copy-start) | copy-done | bytes 1048600
  1.9 0.0 copy-start.1
  1.9 0.9 copy-done.1
  2.9 0.0 copy-start.6
  2.9 0.7 copy-done.6
  3.5 94.0 %shard_map.73 = bf16[1024,512]{1,0:T(8,128)(2,1)S(1)} custom-call(bf16[2,32,16,512]{3,2,1,0:T(8,128)(2,1)S(1)} %bitcast.3, bf16[512,256]{1,0:T(8,128)(2,1)S(1)} %copy-done.1, bf16[2,64]{1,0:T(2,128)(2,1)S(1)} %copy-done.5, f32[200]{0:T(256)S(1)} %copy-done.4, s32[8]{0:T(128)S(1)} %copy-done.6, f32[1,512]{1,0:T(1,128)S(1)} %bitcast.4, s32[1,512]{1,0:T(1,128)S(1)} %bitcast.5), custom_call_target="tpu_custom_call" | custom-call | tf_op jit(solution)/shard_map/pallas_call | solution.py:397
  97.6 1.0 copy.9
Async XLA Ops:
  0.0 0.7 copy-start.3
  0.0 0.7 copy-start.2
  0.0 0.7 copy-start.4
  0.0 0.7 copy-start.5
  0.7 1.2 %copy-start = (bf16[1024,512]{1,0:T(8,128)(2,1)S(1)}, bf16[1024,512]{1,0:T(8,128)(2,1)}, u32[]{:S(2)}) copy-start(bf16[1024,512]{1,0:T(8,128)(2,1)} %param.7) | copy-start | bytes 3145732
  1.9 0.9 copy-start.1
  2.9 0.7 copy-start.6

commit v5 on v4

--- a/solution.py
+++ b/solution.py
@@ -77,15 +77,15 @@
 
 def kernel(
     R, C, amp, fac, lad, occ_e, occ_i, vir_e, vir_m, out,
-    amp_v, lad_v, e_v, m_v, occ_ev, occ_iv,
+    amp_v, stage, lad_v, e_v, m_v, occ_ev, occ_iv,
     comb, factors, part, twin, out1, in1, out2, in2, fit, pairs, hole, hole_in, kron, lad_own,
     lad_all, inverse, coul,
-    loc, fac_s, fac_r, fwd_s, fwd_r, lad_s, lad_r, tw_s, tw_r, s1_s, s1_r, s2_s, s2_r,
+    loc, fac_s, fac_r, fwd_s, fwd_r, hop_s, hop_r, lad_s, lad_r, tw_s, tw_r, s1_s, s1_r, s2_s, s2_r,
     g1_s, g1_r, g2_s, g2_r, rl_s, rl_r, back_s, back_r,
 ):
     nd = R * C
     Z = C // 2
-    occ_row, _, sub, _ = amp.shape
+    occ_row, _, _, sub, _ = amp.shape
     rows = occ_row * VIR
     chunk = rows // C
     q_cols = fac.shape[1]
@@ -105,7 +105,7 @@
         return (lax.div(d, C), lax.rem(d, C))
 
     def peer(o):
-        return lax.rem(r + lax.div(o, C), R) * C + lax.rem(c + lax.rem(o, C), C)
+        return lax.rem(me + o, nd)
 
     def send(src, dst, s, d, target):
         return pltpu.make_async_remote_copy(
@@ -115,7 +115,7 @@
     own_copies = [
         pltpu.make_async_copy(src, dst, loc.at[n])
         for n, (src, dst) in enumerate((
-            (lad, lad_v), (amp, amp_v), (fac, factors.at[r]), (amp.at[:, me], pairs.at[r, :, c]),
+            (lad, lad_v), (amp, amp_v), (fac, factors.at[r]), (amp.at[:, r, c], pairs.at[r, :, c]),
             (vir_e, e_v), (vir_m, m_v), (occ_e, occ_ev), (occ_i, occ_iv),
         ))
     ]
@@ -135,27 +135,38 @@
 
     pl.semaphore_wait(barrier, nd - 1)
 
+    order = [r, r + 1 - 2 * lax.rem(r, 2), lax.rem(r + 2, R), R - 1 - r]
+
     def fac_copy(o):
-        return send(
-            fac, factors.at[r], fac_s.at[o], fac_r.at[r], (lax.rem(r + o, R), c)
-        )
+        return send(fac, factors.at[r], fac_s.at[o], fac_r.at[r], (order[o], c))
 
     for o in range(1, R):
         fac_copy(o).start()
 
+    def col_peer(o):
+        return lax.rem(c + o, C)
+
     def fwd_copy(o):
-        d = peer(o)
-        return send(amp.at[:, d], pairs.at[r, :, c], fwd_s.at[o], fwd_r.at[me], place(d))
+        to = col_peer(o)
+        return send(amp.at[:, :, to], stage.at[c], fwd_s.at[o], fwd_r.at[c], (r, to))
+
+    def hop_copy(src, o):
+        return send(
+            stage.at[src, :, order[o]], pairs.at[r, :, src], hop_s.at[o, src], hop_r.at[r, src],
+            (order[o], c),
+        )
+
+    def own_hop_copy(o):
+        return send(
+            amp.at[:, order[o], c], pairs.at[r, :, c], hop_s.at[o, c], hop_r.at[r, c],
+            (order[o], c),
+        )
 
     def lad_copy(o):
         return send(lad_own, lad_all.at[me], lad_s.at[o], lad_r.at[me], place(peer(o)))
 
-    def fwd_start(lo, hi):
-        @pl.loop(lo, hi)
-        def _(o):
-            fwd_copy(o).start()
-
-    fwd_start(1, C)
+    for o in [C - 1, 1] + list(range(2, C - 1)):
+        fwd_copy(o).start()
 
     own_copies[1].wait()
     for k in range(occ_row):
@@ -189,7 +200,11 @@
             fit.at[src, core], fit.at[src, core], rl_s.at[src], rl_r.at[src], (r, 2 * z + other)
         )
 
-    order = [lax.rem(r + o, R) for o in range(R)]
+    def near_sums(q):
+        tw_copy(q).wait_recv()
+        out1[q, 0] = (part[q, near, core] + twin[q, near]).astype(BF16)
+        out1[q, 1] = (part[q, far_near, core] + twin[q, far_near]).astype(BF16)
+        s1_copy(q).start()
 
     for o, q in enumerate(order):
         if o:
@@ -197,18 +212,25 @@
         got = jnp.dot(comb[...], factors[q], preferred_element_type=F32)
         part[q] = got.reshape(Z, 2, chunk, q_cols)
         tw_copy(q).start()
-        if o == 0:
-            fwd_start(C, nd)
-
-            @pl.loop(1, nd)
-            def _(n):
-                lad_copy(n).start()
-
-    for q in order:
-        tw_copy(q).wait_recv()
-        out1[q, 0] = (part[q, near, core] + twin[q, near]).astype(BF16)
-        out1[q, 1] = (part[q, far_near, core] + twin[q, far_near]).astype(BF16)
-        s1_copy(q).start()
+        if o:
+            near_sums(order[o - 1])
+    for o in range(1, R):
+        own_hop_copy(o).start()
+    near_sums(order[R - 1])
+
+    @pl.loop(1, nd)
+    def _(n):
+        lad_copy(n).start()
+
+    @pl.loop(1, C)
+    def _(n):
+        src = lax.rem(c + n, C)
+        send(
+            amp.at[:, :, c], stage.at[src], fwd_s.at[n], fwd_r.at[src], (r, src)
+        ).wait_recv()
+        for o in range(1, R):
+            hop_copy(src, o).start()
+        pairs[r, :, src] = stage[src, :, r]
 
     for copy in own_copies[4:]:
         copy.wait()
@@ -251,13 +273,19 @@
         )
         kron[pl.ds(at, step_rows), :] = jnp.where(same, block, 0.0).astype(BF16)
 
+    for q in order:
+        s1_copy(q).wait_recv()
+        out2[q] = ((part[q, far, core] + twin[q, far]) + in1[q, 1].astype(F32)).astype(BF16)
+        s2_copy(q).start()
+
     own_copies[3].wait()
-
-    @pl.loop(1, nd)
-    def _(o):
-        d = peer(o)
-        dr, dc = place(d)
-        send(amp.at[:, d], pairs.at[dr, :, dc], fwd_s.at[o], fwd_r.at[d], (dr, dc)).wait_recv()
+    for o in range(1, R):
+        @pl.loop(0, C)
+        def _(src):
+            send(
+                stage.at[src, :, r], pairs.at[order[o], :, src], hop_s.at[o, src],
+                hop_r.at[order[o], src], (order[o], c),
+            ).wait_recv()
 
     row_blocks = wide // R
     for n in range(R):
@@ -273,14 +301,9 @@
         dr, dc = place(d)
         return send(hole.at[dr, :, dc], hole_in.at[:, me], back_s.at[o], back_r.at[me], (dr, dc))
 
-    @pl.loop(1, nd)
+    @pl.loop(1, nd // 2)
     def _(o):
         back_copy(o).start()
-
-    for q in order:
-        s1_copy(q).wait_recv()
-        out2[q] = ((part[q, far, core] + twin[q, far]) + in1[q, 1].astype(F32)).astype(BF16)
-        s2_copy(q).start()
 
     hole_in[:, me] = hole[r, :, c]
 
@@ -291,6 +314,11 @@
         g1_copy(q).start()
         g2_copy(0, q).start()
     relay(z).start()
+
+    @pl.loop(nd // 2, nd)
+    def _(o):
+        back_copy(o).start()
+
 
     def g1_wait(q):
         send(
@@ -363,12 +391,17 @@
 
     @pl.loop(1, nd)
     def _(o):
-        fwd_copy(o).wait_send()
         lad_copy(o).wait_send()
         back_copy(o).wait_send()
 
+    for o in range(1, C):
+        fwd_copy(o).wait_send()
     for o in range(1, R):
         fac_copy(o).wait_send()
+
+        @pl.loop(0, C)
+        def _(src):
+            hop_copy(src, o).wait_send()
     for q in range(R):
         tw_copy(q).wait_send()
         s1_copy(q).wait_send()
@@ -400,7 +433,8 @@
         in_specs=[hbm] * 7,
         out_specs=pl.BlockSpec(memory_space=pltpu.VMEM),
         scratch_shapes=[
-            pltpu.VMEM((occ_row, nd, sub, VIR), BF16),
+            pltpu.VMEM((occ_row, R, C, sub, VIR), BF16),
+            pltpu.VMEM((C, occ_row, R, sub, VIR), BF16),
             pltpu.VMEM(ladder.shape, BF16),
             pltpu.VMEM((1, VIR), F32),
             pltpu.VMEM((1, VIR), jnp.int32),
@@ -425,7 +459,8 @@
             pltpu.VMEM((4, chunk, VIR), F32),
             dma((8,)),
             dma((R,)), dma((R,)),
-            dma((nd,)), dma((nd,)),
+            dma((C,)), dma((C,)),
+            dma((R, C)), dma((R, C)),
             dma((nd,)), dma((nd,)),
             dma((R,)), dma((R,)),
             dma((R,)), dma((R,)),
@@ -436,10 +471,10 @@
             dma((nd,)), dma((nd,)),
         ],
         compiler_params=pltpu.CompilerParams(
-            collective_id=0, has_side_effects=True, vmem_limit_bytes=40 * 2**20
+            collective_id=0, has_side_effects=True, vmem_limit_bytes=56 * 2**20
         ),
     )(
-        amplitudes.reshape(occ_row, nd, sub, VIR), df_factors, ladder, occ_energy, occ_index,
+        amplitudes.reshape(occ_row, R, C, sub, VIR), df_factors, ladder, occ_energy, occ_index,
         vir_energy.reshape(1, VIR), vir_map.reshape(1, VIR),
     )
 
@@ -450,7 +485,7 @@
     fits = (
         VIR % (16 * R * C) == 0
         and cols == VIR
-        and C == 8
+        and (R, C) == (4, 8)
         and rows % (16 * C) == 0
         and VIR % (rows // C) == 0
         and (rows // C) % (VIR // (R * C)) == 0

time: 98.8 us -> 97.6 us (0.988)
  local copies, waits for them, and re-layouts: 4.51 us -> 2.26 us
  Pallas kernels: 94 us -> 95.2 us
    unnamed x15 -> x1, local copies, waits for them, and re-layouts: 4.51 us -> 2.26 us
    pallas_call x1, Pallas kernels: 94 us -> 95.2 us  [fused(): pl.pallas_call(functools.partial(kernel, R, C), out_shape=jax.ShapeDtypeS...]
where the time goes in v5:
time: 97.6 us; the launch traced here: 97.4 us
  Pallas kernels  95.2 us (98%)
  local copies, waits for them, and re-layouts  2.26 us (2%)
    pallas_call x1, Pallas kernels, fused(): pl.pallas_call(functools.partial(kernel, R, C), out_shape=jax.ShapeDtypeS...  95.2 us
    unnamed x1, local copies, waits for them, and re-layouts  2.26 us

profile of v5, /device:TPU:0, one launch (start us, length us, event | category | flops | bytes accessed | tf_op | source)
XLA Modules:
  0.0 97.4 jit_solution(2801530043462858777)
XLA Ops:
  0.0 95.2 %shard_map.73 = bf16[1024,512]{1,0:T(8,128)(2,1)} custom-call(bf16[2,4,8,16,512]{4,3,2,1,0:T(8,128)(2,1)} %bitcast.3, bf16[512,256]{1,0:T(8,128)(2,1)} %fac.1, bf16[2,64]{1,0:T(2,128)(2,1)} %lad.1, f32[200]{0:T(256)} %occ_e.1, s32[8]{0:T(128)} %occ_i.1, f32[1,512]{1,0:T(1,128)} %bitcast.4, s32[1,512]{1,0:T(1,128)} %bitcast.5), custom_call_target="tpu_custom_call" | custom-call | tf_op jit(solution)/shard_map/pallas_call | solution.py:430
  95.2 2.3 %copy.9 = bf16[1024,512]{1,0:T(8,128)(2,1)} copy(bf16[1024,512]{1,0:T(8,128)(2,1)} %shard_map.73) | data formatting | bytes 2097152

commit v6 on v4

--- a/solution.py
+++ b/solution.py
@@ -78,7 +78,7 @@
 def kernel(
     R, C, amp, fac, lad, occ_e, occ_i, vir_e, vir_m, out,
     amp_v, lad_v, e_v, m_v, occ_ev, occ_iv,
-    comb, factors, part, twin, out1, in1, out2, in2, fit, pairs, hole, hole_in, kron, lad_own,
+    comb, factors, turned, part, away, twin, out1, in1, out2, in2, fit, pairs, hole, hole_in, kron, lad_own,
     lad_all, inverse, coul,
     loc, fac_s, fac_r, fwd_s, fwd_r, lad_s, lad_r, tw_s, tw_r, s1_s, s1_r, s2_s, s2_r,
     g1_s, g1_r, g2_s, g2_r, rl_s, rl_r, back_s, back_r,
@@ -105,7 +105,7 @@
         return (lax.div(d, C), lax.rem(d, C))
 
     def peer(o):
-        return lax.rem(r + lax.div(o, C), R) * C + lax.rem(c + lax.rem(o, C), C)
+        return lax.rem(me + o, nd)
 
     def send(src, dst, s, d, target):
         return pltpu.make_async_remote_copy(
@@ -135,10 +135,10 @@
 
     pl.semaphore_wait(barrier, nd - 1)
 
+    order = [r, r + 1 - 2 * lax.rem(r, 2), lax.rem(r + 2, R), R - 1 - r]
+
     def fac_copy(o):
-        return send(
-            fac, factors.at[r], fac_s.at[o], fac_r.at[r], (lax.rem(r + o, R), c)
-        )
+        return send(fac, factors.at[r], fac_s.at[o], fac_r.at[r], (order[o], c))
 
     for o in range(1, R):
         fac_copy(o).start()
@@ -155,7 +155,11 @@
         def _(o):
             fwd_copy(o).start()
 
-    fwd_start(1, C)
+    @pl.loop(1, nd)
+    def _(n):
+        lad_copy(n).start()
+
+    fwd_start(1, nd)
 
     own_copies[1].wait()
     for k in range(occ_row):
@@ -164,7 +168,7 @@
     own_copies[2].wait()
 
     def tw_copy(q):
-        return send(part.at[q, :, other], twin.at[q], tw_s.at[q], tw_r.at[q], (r, 2 * z + other))
+        return send(away.at[q], twin.at[q], tw_s.at[q], tw_r.at[q], (r, 2 * z + other))
 
     def s1_copy(q):
         return send(out1.at[q], in1.at[q], s1_s.at[q], s1_r.at[q], (r, 2 * near + core))
@@ -189,26 +193,23 @@
             fit.at[src, core], fit.at[src, core], rl_s.at[src], rl_r.at[src], (r, 2 * z + other)
         )
 
-    order = [lax.rem(r + o, R) for o in range(R)]
-
-    for o, q in enumerate(order):
-        if o:
-            send(fac, factors.at[q], fac_s.at[o], fac_r.at[q], (r, c)).wait_recv()
+    def partial_sums(q):
         got = jnp.dot(comb[...], factors[q], preferred_element_type=F32)
-        part[q] = got.reshape(Z, 2, chunk, q_cols)
+        got = got.reshape(Z, 2, chunk, q_cols)
+        part[q] = got
+        away[q] = part[q, :, other].astype(BF16)
         tw_copy(q).start()
-        if o == 0:
-            fwd_start(C, nd)
-
-            @pl.loop(1, nd)
-            def _(n):
-                lad_copy(n).start()
-
-    for q in order:
+
+    def pair_sum(q, to):
+        return part[q, to, core] + twin[q, to].astype(F32)
+
+    def near_sums(q):
         tw_copy(q).wait_recv()
-        out1[q, 0] = (part[q, near, core] + twin[q, near]).astype(BF16)
-        out1[q, 1] = (part[q, far_near, core] + twin[q, far_near]).astype(BF16)
+        out1[q, 0] = pair_sum(q, near).astype(BF16)
+        out1[q, 1] = pair_sum(q, far_near).astype(BF16)
         s1_copy(q).start()
+
+    partial_sums(r)
 
     for copy in own_copies[4:]:
         copy.wait()
@@ -222,6 +223,8 @@
         energy = occ_ev[occ_iv[r * occ_row + k]] + energy_j
         inverse[k * VIR:(k + 1) * VIR, :] = 1.0 / ((energy - v_col) - v_row)
 
+    near_sums(r)
+
     @pl.loop(1, nd)
     def _(o):
         d = peer(o)
@@ -251,6 +254,22 @@
         )
         kron[pl.ds(at, step_rows), :] = jnp.where(same, block, 0.0).astype(BF16)
 
+    for o in range(1, R):
+        q = order[o]
+        send(fac, factors.at[q], fac_s.at[o], fac_r.at[q], (r, c)).wait_recv()
+        partial_sums(q)
+        if o > 1:
+            near_sums(order[o - 1])
+    near_sums(order[R - 1])
+
+    for q in range(R):
+        turned[q] = factors[q].T
+
+    for q in order:
+        s1_copy(q).wait_recv()
+        out2[q] = (pair_sum(q, far) + in1[q, 1].astype(F32)).astype(BF16)
+        s2_copy(q).start()
+
     own_copies[3].wait()
 
     @pl.loop(1, nd)
@@ -273,24 +292,23 @@
         dr, dc = place(d)
         return send(hole.at[dr, :, dc], hole_in.at[:, me], back_s.at[o], back_r.at[me], (dr, dc))
 
-    @pl.loop(1, nd)
+    @pl.loop(1, nd // 2)
     def _(o):
         back_copy(o).start()
-
-    for q in order:
-        s1_copy(q).wait_recv()
-        out2[q] = ((part[q, far, core] + twin[q, far]) + in1[q, 1].astype(F32)).astype(BF16)
-        s2_copy(q).start()
 
     hole_in[:, me] = hole[r, :, c]
 
     for q in order:
         s2_copy(q).wait_recv()
-        total = (part[q, z, core] + twin[q, z]) + in1[q, 0].astype(F32)
+        total = pair_sum(q, z) + in1[q, 0].astype(F32)
         fit[z, core, q] = (total + in2[q].astype(F32)).astype(BF16)
         g1_copy(q).start()
         g2_copy(0, q).start()
     relay(z).start()
+
+    @pl.loop(nd // 2, nd)
+    def _(o):
+        back_copy(o).start()
 
     def g1_wait(q):
         send(
@@ -313,10 +331,7 @@
     def fitted_dot(src, which):
         acc = None
         for q in range(R):
-            term = lax.dot_general(
-                fit[src, which, q], factors[q], (((1,), (1,)), ((), ())),
-                preferred_element_type=F32,
-            )
+            term = jnp.dot(fit[src, which, q], turned[q], preferred_element_type=F32)
             acc = term if acc is None else acc + term
         return acc
 
@@ -408,8 +423,10 @@
             pltpu.SMEM(occ_index.shape, jnp.int32),
             pltpu.VMEM((rows, VIR), BF16),
             pltpu.VMEM((R, depth, q_cols), BF16),
+            pltpu.VMEM((R, q_cols, depth), BF16),
             pltpu.VMEM((R, Z, 2, chunk, q_cols), F32),
-            pltpu.VMEM((R, Z, chunk, q_cols), F32),
+            pltpu.VMEM((R, Z, chunk, q_cols), BF16),
+            pltpu.VMEM((R, Z, chunk, q_cols), BF16),
             pltpu.VMEM((R, 2, chunk, q_cols), BF16),
             pltpu.VMEM((R, 2, chunk, q_cols), BF16),
             pltpu.VMEM((R, chunk, q_cols), BF16),
@@ -436,7 +453,7 @@
             dma((nd,)), dma((nd,)),
         ],
         compiler_params=pltpu.CompilerParams(
-            collective_id=0, has_side_effects=True, vmem_limit_bytes=40 * 2**20
+            collective_id=0, has_side_effects=True, vmem_limit_bytes=56 * 2**20
         ),
     )(
         amplitudes.reshape(occ_row, nd, sub, VIR), df_factors, ladder, occ_energy, occ_index,
@@ -450,7 +467,7 @@
     fits = (
         VIR % (16 * R * C) == 0
         and cols == VIR
-        and C == 8
+        and (R, C) == (4, 8)
         and rows % (16 * C) == 0
         and VIR % (rows // C) == 0
         and (rows // C) % (VIR // (R * C)) == 0

time: 98.8 us -> 99.3 us (level)
  the two profiles are of different devices: /device:TPU:0 before, /device:TPU:11 now
where the time goes in v6:
time: 99.3 us; the launch traced here: 99.2 us
  Pallas kernels  96.9 us (98%)
  local copies, waits for them, and re-layouts  2.26 us (2%)
    pallas_call x1, Pallas kernels, fused(): pl.pallas_call(functools.partial(kernel, R, C), out_shape=jax.ShapeDtypeS...  96.9 us
    unnamed x1, local copies, waits for them, and re-layouts  2.26 us

profile of v6, /device:TPU:11, one launch (start us, length us, event | category | flops | bytes accessed | tf_op | source)
XLA Modules:
  0.0 99.2 jit_solution(17934098660848347927)
XLA Ops:
  0.0 96.9 %shard_map.73 = bf16[1024,512]{1,0:T(8,128)(2,1)} custom-call(bf16[2,32,16,512]{3,2,1,0:T(8,128)(2,1)} %bitcast.3, bf16[512,256]{1,0:T(8,128)(2,1)} %fac.1, bf16[2,64]{1,0:T(2,128)(2,1)} %lad.1, f32[200]{0:T(256)} %occ_e.1, s32[8]{0:T(128)} %occ_i.1, f32[1,512]{1,0:T(1,128)} %bitcast.4, s32[1,512]{1,0:T(1,128)} %bitcast.5), custom_call_target="tpu_custom_call" | custom-call | tf_op jit(solution)/shard_map/pallas_call | solution.py:412
  96.9 2.3 %copy.9 = bf16[1024,512]{1,0:T(8,128)(2,1)} copy(bf16[1024,512]{1,0:T(8,128)(2,1)} %shard_map.73) | data formatting | bytes 2097152

commit v7 on v6

--- a/solution.py
+++ b/solution.py
@@ -79,7 +79,7 @@
     R, C, amp, fac, lad, occ_e, occ_i, vir_e, vir_m, out,
     amp_v, lad_v, e_v, m_v, occ_ev, occ_iv,
     comb, factors, turned, part, away, twin, out1, in1, out2, in2, fit, pairs, hole, hole_in, kron, lad_own,
-    lad_all, inverse, coul,
+    lad_all, inverse, coul, held_sum,
     loc, fac_s, fac_r, fwd_s, fwd_r, lad_s, lad_r, tw_s, tw_r, s1_s, s1_r, s2_s, s2_r,
     g1_s, g1_r, g2_s, g2_r, rl_s, rl_r, back_s, back_r,
 ):
@@ -262,41 +262,55 @@
             near_sums(order[o - 1])
     near_sums(order[R - 1])
 
-    for q in range(R):
-        turned[q] = factors[q].T
+    own_copies[3].wait()
+    row_blocks = wide // R
+    for o in range(R):
+        source = lax.rem(r + R - o, R)
+
+        @pl.loop(0 if o else 1, C)
+        def _(n):
+            dc = lax.rem(c + n, C)
+            d = source * C + dc
+            send(
+                amp.at[:, d], pairs.at[source, :, dc], fwd_s.at[n], fwd_r.at[d], (source, dc)
+            ).wait_recv()
+
+        block = pairs[source].reshape(row_blocks, VIR)
+        at = pl.multiple_of(source * row_blocks, row_blocks)
+        for n in range(R):
+            rows_n = slice(n * row_blocks, (n + 1) * row_blocks)
+            term = jnp.dot(
+                kron[rows_n, pl.ds(at, row_blocks)], block, preferred_element_type=F32
+            )
+            if o:
+                term = held_sum[rows_n, :] + term
+            if o < R - 1:
+                held_sum[rows_n, :] = term
+            else:
+                hole[n] = term.astype(BF16).reshape(occ_row, C, sub, VIR)
+
+    def back_copy(o):
+        d = peer(o)
+        dr, dc = place(d)
+        return send(hole.at[dr, :, dc], hole_in.at[:, me], back_s.at[o], back_r.at[me], (dr, dc))
+
+    @pl.loop(1, nd // 2)
+    def _(o):
+        back_copy(o).start()
 
     for q in order:
         s1_copy(q).wait_recv()
         out2[q] = (pair_sum(q, far) + in1[q, 1].astype(F32)).astype(BF16)
         s2_copy(q).start()
 
-    own_copies[3].wait()
-
-    @pl.loop(1, nd)
-    def _(o):
-        d = peer(o)
-        dr, dc = place(d)
-        send(amp.at[:, d], pairs.at[dr, :, dc], fwd_s.at[o], fwd_r.at[d], (dr, dc)).wait_recv()
-
-    row_blocks = wide // R
-    for n in range(R):
-        term = jnp.dot(
-            kron[n * row_blocks:(n + 1) * row_blocks, :],
-            pairs[...].reshape(wide, VIR),
-            preferred_element_type=F32,
-        )
-        hole[n] = term.astype(BF16).reshape(occ_row, C, sub, VIR)
-
-    def back_copy(o):
-        d = peer(o)
-        dr, dc = place(d)
-        return send(hole.at[dr, :, dc], hole_in.at[:, me], back_s.at[o], back_r.at[me], (dr, dc))
-
-    @pl.loop(1, nd // 2)
+    @pl.loop(nd // 2, nd)
     def _(o):
         back_copy(o).start()
 
     hole_in[:, me] = hole[r, :, c]
+    for q in range(R):
+        turned[q] = factors[q].T
+
 
     for q in order:
         s2_copy(q).wait_recv()
@@ -305,10 +319,6 @@
         g1_copy(q).start()
         g2_copy(0, q).start()
     relay(z).start()
-
-    @pl.loop(nd // 2, nd)
-    def _(o):
-        back_copy(o).start()
 
     def g1_wait(q):
         send(
@@ -440,6 +450,7 @@
             pltpu.VMEM((nd, lad_rows, lad_cols), F32),
             pltpu.VMEM((rows, VIR), F32),
             pltpu.VMEM((4, chunk, VIR), F32),
+            pltpu.VMEM((wide, VIR), F32),
             dma((8,)),
             dma((R,)), dma((R,)),
             dma((nd,)), dma((nd,)),

time: 99.3 us -> 98 us (0.987)
  the two profiles are of different devices: /device:TPU:11 before, /device:TPU:0 now
where the time goes in v7:
time: 98 us; the launch traced here: 97.3 us
  Pallas kernels  95 us (97%)
  local copies, waits for them, and re-layouts  2.26 us (2%)
    pallas_call x1, Pallas kernels, fused(): pl.pallas_call(functools.partial(kernel, R, C), out_shape=jax.ShapeDtypeS...  95 us
    unnamed x1, local copies, waits for them, and re-layouts  2.26 us

profile of v7, /device:TPU:0, one launch (start us, length us, event | category | flops | bytes accessed | tf_op | source)
XLA Modules:
  0.0 97.3 jit_solution(8740824786035354176)
XLA Ops:
  0.0 95.0 %shard_map.73 = bf16[1024,512]{1,0:T(8,128)(2,1)} custom-call(bf16[2,32,16,512]{3,2,1,0:T(8,128)(2,1)} %bitcast.3, bf16[512,256]{1,0:T(8,128)(2,1)} %fac.1, bf16[2,64]{1,0:T(2,128)(2,1)} %lad.1, f32[200]{0:T(256)} %occ_e.1, s32[8]{0:T(128)} %occ_i.1, f32[1,512]{1,0:T(1,128)} %bitcast.4, s32[1,512]{1,0:T(1,128)} %bitcast.5), custom_call_target="tpu_custom_call" | custom-call | tf_op jit(solution)/shard_map/pallas_call | solution.py:422
  95.0 2.3 %copy.9 = bf16[1024,512]{1,0:T(8,128)(2,1)} copy(bf16[1024,512]{1,0:T(8,128)(2,1)} %shard_map.73) | data formatting | bytes 2097152
